TPU v7x, 32 devices: a whole 2x2x4 slice. The times are simulated.
32 devices in a mesh: contact: 8 (over y, x, core), body: 4 (over z).
Axes of the slice: x: 2, y: 2, z: 4, core: 2. Of those that a mesh axis runs over, the one named last changes fastest.
Arguments:
- jacobian: bfloat16 [512, 2, 384, 384], P(('contact', 'body')), may hold values from -0.21875 to 0.21875
- tile_block: int32 [512, 2], P(('contact', 'body')), may hold values from 0 to 31
- tile_count: int32 [32], P(('contact', 'body')), may hold values from 8 to 16, as said below
- vel_free: float32 [128, 384], P('body'), may hold values from -6 to 6
- inv_mass: float32 [128, 384], P('body'), may hold values from 0.25 to 2
- bias: float32 [512, 384], P(('contact', 'body')), may hold values from -6 to 6
- step_scale: float32 [512, 384], P(('contact', 'body')), may hold values from 0.05 to 0.5
- friction: float32 [512, 128], P(('contact', 'body')), may hold values from 0.2 to 1
- impulse_start: float32 [512, 384], P(('contact', 'body')), may hold values from -6 to 6
Outputs:
- impulse: float32 [512, 384], P(('contact', 'body'))
- velocity: float32 [128, 384], P('body')
Inputs may be any that keep to these rules, and one draw needn't show every extreme that they name: `tile_count`: some device has all 16 tile slots live in every draw.
All inputs are finite; a program needn't handle non-finite values.
Results may differ from a plain program's by a relative error of at most 0.0062.
Values may be sent and summed in bfloat16 or wider, within the bound.
No kernel may reach another device: no remote copies, remote signals or barrier semaphores. Data moves between devices by JAX's collectives and lax.ppermute only.
A program may use at most 64 MiB of HBM per device.

v0:
```python
import jax
import jax.numpy as jnp
from jax import lax
from jax.experimental import pallas as pl
from jax.experimental.pallas import tpu as pltpu
from jax.sharding import PartitionSpec as P

ITERS = 2


def shifted(value, axis, steps):
    count = lax.axis_size(axis)
    pairs = [(source, (source + steps) % count) for source in range(count)]
    return lax.ppermute(value, axis, pairs)


def crossed(value, target):
    count, groups = lax.axis_size("body"), lax.axis_size("contact")
    cross = 1 if groups % 2 == 0 else 0
    pairs = [
        (group * count + place, (group ^ cross) * count + target(place) % count)
        for group in range(groups)
        for place in range(count)
    ]
    return lax.ppermute(value, ("contact", "body"), pairs)


def ahead_of(place):
    return place + 1


def traded(ahead, back, even):
    if lax.axis_size("body") % 2:
        return crossed(ahead, ahead_of), crossed(back, lambda place: place - 1)
    wide = crossed(jnp.where(even, back, ahead), lambda place: place + 2 * (place % 2) - 1)
    near = crossed(jnp.where(even, ahead, back), lambda place: place ^ 1)
    return jnp.where(even, wide, near), jnp.where(even, near, wide)


def rounded(value):
    return value.astype(jnp.bfloat16)


def tree(values):
    while len(values) > 1:
        values = [left + right for left, right in zip(values[::2], values[1::2])]
    return values[0]


def pair_sum(value):
    count = lax.axis_size("contact")
    if count % 2:
        return value
    return value + lax.ppermute(value, "contact", [(place, place ^ 1) for place in range(count)])


def over_pairs(value):
    count = lax.axis_size("contact")
    if count & (count - 1):
        mine = (lax.axis_index("contact") & 1) == 0
        return lax.psum(value if count % 2 else jnp.where(mine, value, 0.0), "contact")
    stride = 2
    while stride < count:
        radix = min(count // stride, 4)
        parts = []
        for digit in range(1, radix):
            pairs = [(place, place ^ (digit * stride) ^ 1) for place in range(count)]
            parts.append(lax.ppermute(rounded(value), "contact", pairs))
        parts.append(rounded(value))
        value = tree([part.astype(jnp.float32) for part in parts])
        stride *= radix
    return value


def project(trial, friction, contacts):
    normal = trial[:, :contacts]
    first = trial[:, contacts : 2 * contacts]
    second = trial[:, 2 * contacts :]
    tangent = jnp.sqrt(first * first + second * second)
    inside = tangent <= friction * normal
    below = friction * tangent <= -normal
    moved = (normal + friction * tangent) / (1.0 + friction * friction)
    safe = jnp.where(inside | below, 1.0, tangent)
    factor = jnp.where(inside, 1.0, jnp.where(below, 0.0, friction * moved / safe))
    new_normal = jnp.where(inside, normal, jnp.where(below, 0.0, moved))
    return jnp.concatenate([new_normal, first * factor, second * factor], axis=1)


def push_tile(tile, lam_ref, turned_ref, block_ref, sums_ref):
    blocks, dofs = sums_ref.shape[0] // 2, sums_ref.shape[1]
    row = jnp.broadcast_to(lam_ref[pl.ds(tile, 1), :], (16, lam_ref.shape[1]))
    push = jnp.dot(
        row.astype(jnp.bfloat16), turned_ref[tile], preferred_element_type=jnp.float32
    )
    sums_ref[pl.ds(block_ref[0, tile], 1), :] += push[:1, :dofs]
    sums_ref[pl.ds(blocks + block_ref[1, tile], 1), :] += push[:1, dofs:]


def first_kernel(
    count_ref, block_ref, jac_ref, start_ref, kept_ref, turned_ref, live_ref, lam_ref, sums_ref,
    block, sems, small_sems,
):
    tiles = start_ref.shape[0]
    small = [
        pltpu.make_async_copy(source, target, small_sems.at[place])
        for place, (source, target) in enumerate(
            [(block_ref, block), (start_ref, lam_ref)]
        )
    ]
    copies = [
        pltpu.make_async_copy(jac_ref.at[tile], kept_ref.at[tile], sems.at[tile])
        for tile in range(tiles)
    ]
    groups = [range(first, min(first + GROUP, tiles)) for first in range(0, tiles, GROUP)]
    for copy in small + copies[: 2 * GROUP]:
        copy.start()
    sums_ref[...] = jnp.zeros_like(sums_ref)
    for copy in small:
        copy.wait()
    order = lax.broadcasted_iota(jnp.int32, lam_ref.shape, 0)
    live_ref[...] = jnp.where(order < count_ref[0], 1.0, 0.0)
    lam_ref[...] = lam_ref[...] * live_ref[...]
    for group in groups:
        for tile in group:
            copies[tile].wait()
        for copy in copies[group[0] + 2 * GROUP : group[0] + 3 * GROUP]:
            copy.start()
        for tile in group:
            turned_ref[tile] = kept_ref[tile].T
        for tile in group:
            push_tile(tile, lam_ref, turned_ref, block, sums_ref)


def sweep_kernel(
    block_ref, live_ref, jac_ref, turned_ref, free_ref, mass_ref, beside_ref,
    bias_ref, step_ref, friction_ref, old_ref, total_ref,
    lam_ref, sums_ref, vel_ref, rel_ref,
):
    tiles = old_ref.shape[0]
    blocks, dofs = free_ref.shape
    total = total_ref[...]
    own_vel = free_ref[...] + mass_ref[...] * total[:blocks]
    next_vel = beside_ref[:blocks] + beside_ref[blocks:] * total[blocks:]
    vel_ref[:, :dofs] = own_vel
    vel_ref[:, dofs:] = next_vel
    sums_ref[...] = jnp.zeros_like(sums_ref)
    for tile in range(tiles):
        own_row = vel_ref[pl.ds(block_ref[0, tile], 1), :dofs]
        next_row = vel_ref[pl.ds(block_ref[1, tile], 1), dofs:]
        row = jnp.broadcast_to(jnp.concatenate([own_row, next_row], axis=1), (16, 2 * dofs))
        rel = jnp.dot(row.astype(jnp.bfloat16), jac_ref[tile], preferred_element_type=jnp.float32)
        rel_ref[pl.ds(tile, 1), :] = rel[:1]
    trial = old_ref[...] - step_ref[...] * (rel_ref[...] + bias_ref[...])
    lam = project(trial, friction_ref[...], friction_ref.shape[1])
    lam_ref[...] = lam * live_ref[...]
    for tile in range(tiles):
        push_tile(tile, lam_ref, turned_ref, block_ref, sums_ref)


GROUP = 4
LIMIT = 24 * 1024 * 1024
SMEM = pl.BlockSpec(memory_space=pltpu.SMEM)
VMEM = pl.BlockSpec(memory_space=pltpu.VMEM)


def result_shapes(lam, blocks, dofs):
    return [
        jax.ShapeDtypeStruct(lam.shape, jnp.float32),
        jax.ShapeDtypeStruct((2 * blocks, dofs), jnp.float32),
    ]


def first_push(jacobian, tile_block, tile_count, start, blocks):
    tiles, rows, cols = jacobian.shape
    lam_shape, sums_shape = result_shapes(start, blocks, rows // 2)
    held = [
        pltpu.with_memory_space_constraint(array, pltpu.HBM)
        for array in (tile_block, jacobian, start)
    ]
    return pl.pallas_call(
        first_kernel,
        out_shape=[
            pltpu.VMEM((tiles, rows, cols), jacobian.dtype),
            pltpu.VMEM((tiles, cols, rows), jacobian.dtype),
            lam_shape, lam_shape, sums_shape,
        ],
        in_specs=[SMEM] + [pl.BlockSpec(memory_space=pltpu.HBM)] * 3,
        out_specs=[VMEM] * 5,
        scratch_shapes=[
            pltpu.SMEM(tile_block.shape, jnp.int32),
            pltpu.SemaphoreType.DMA((tiles,)),
            pltpu.SemaphoreType.DMA((2,)),
        ],
        compiler_params=pltpu.CompilerParams(vmem_limit_bytes=LIMIT),
        cost_estimate=pl.CostEstimate(
            flops=2 * jacobian.size, bytes_accessed=2 * jacobian.size, transcendentals=0
        ),
        name="first_push",
    )(tile_count, *held)


def sweep_step(kept, turned, tile_block, live, free, mass, beside, bias, step, friction, lam, total):
    blocks, dofs = free.shape
    kept = pltpu.with_memory_space_constraint(kept, pltpu.VMEM)
    turned = pltpu.with_memory_space_constraint(turned, pltpu.VMEM)
    return pl.pallas_call(
        sweep_kernel,
        out_shape=result_shapes(lam, blocks, dofs),
        in_specs=[SMEM] + [VMEM] * 11,
        out_specs=[VMEM] * 2,
        scratch_shapes=[
            pltpu.VMEM((blocks, 2 * dofs), jnp.float32),
            pltpu.VMEM(lam.shape, jnp.float32),
        ],
        compiler_params=pltpu.CompilerParams(vmem_limit_bytes=LIMIT),
        cost_estimate=pl.CostEstimate(
            flops=4 * kept.size, bytes_accessed=4 * kept.size, transcendentals=0
        ),
        name="sweep_step",
    )(tile_block, live, kept, turned, free, mass, beside, bias, step, friction, lam, total)


def per_device(
    jacobian, tile_block, tile_count, vel_free, inv_mass, bias, step_scale, friction, impulse_start
):
    tiles, sides, dofs, rows = jacobian.shape
    blocks = vel_free.shape[0]
    flat = jacobian.reshape(tiles, sides * dofs, rows)
    even = (lax.axis_index("body") & 1) == 0
    even, tile_block = lax.optimization_barrier((even, tile_block.T))
    beside = shifted(jnp.concatenate([vel_free, inv_mass]), "body", -1)
    kept, turned, live, lam, sums = first_push(flat, tile_block, tile_count, impulse_start, blocks)
    beside, sums = lax.optimization_barrier((beside, sums))
    for sweep in range(ITERS):
        both = pair_sum(sums)
        own, later = both[:blocks], both[blocks:]
        from_last, from_next = traded(rounded(later), rounded(own), even)
        total = over_pairs(jnp.concatenate([own + from_last, later + from_next]))
        lam, sums = sweep_step(
            kept, turned, tile_block, live, vel_free, inv_mass, beside,
            bias, step_scale, friction, lam, total,
        )
    both = pair_sum(sums)
    from_last = crossed(rounded(both[blocks:]), ahead_of)
    total = over_pairs(both[:blocks] + from_last)
    velocity = vel_free + inv_mass * total
    return (lam, velocity)


def solution(mesh):
    placed = (
        P(("contact", "body"), None, None, None),
        P(("contact", "body"), None),
        P(("contact", "body")),
        P("body", None),
        P("body", None),
        P(("contact", "body"), None),
        P(("contact", "body"), None),
        P(("contact", "body"), None),
        P(("contact", "body"), None),
    )
    return jax.shard_map(
        per_device,
        mesh=mesh,
        in_specs=placed,
        out_specs=(P(("contact", "body"), None), P("body", None)),
        check_vma=False,
    )
```

profile of v0, /device:TPU:0, one launch (start us, length us, event | category | flops | bytes accessed | tf_op | source)
XLA Modules:
  0.0 58.1 jit_solution(16002164983006367057)
XLA Ops:
  0.6 0.0 copy-start.1
  0.6 0.0 copy-start
  0.7 0.0 copy-start.5
  0.7 0.0 copy-start.4
  0.7 0.0 copy-start.3
  0.7 0.0 copy-start.2
  0.7 0.9 %pad_maximum_fusion = f32[64,384]{1,0:T(8,128)S(1)} fusion(f32[32,384]{1,0:T(8,128)} %mass_ref.3, f32[32,384]{1,0:T(8,128)} %free_ref.3), kind=kLoop, calls=%fused_computation | loop fusion | flops 24576 | bytes 196608 | tf_op jit(solution)/shard_map/concatenate | solution.py:231
  1.6 5.1 %collective-permute-start = (f32[64,384]{1,0:T(8,128)S(1)}, f32[64,384]{1,0:T(8,128)S(1)}, u32[]{:S(2)}, u32[]{:S(2)}) collective-permute-start(f32[64,384]{1,0:T(8,128)S(1)} %pad_maximum_fusion), channel_id=1, source_target_pairs={{0,3},{1,0},{2,1},{3,2},{4,7},{5,4},{6,5},{7,6},{8,11},{9,8},{10,9... | collective-permute-start | bytes 294920 | tf_op jit(solution)/shard_map/ppermute | solution.py:14
  7.3 5.5 %first_push.1 = (bf16[16,768,384]{2,1,0:T(8,128)(2,1)S(1)}, bf16[16,384,768]{2,1,0:T(8,128)(2,1)S(1)}, f32[16,384]{1,0:T(8,128)S(1)}, f32[16,384]{1,0:T(8,128)S(1)}, f32[64,384]{1,0:T(8,128)S(1)}) custom-call(s32[1]{0:T(128)S(6)} %copy.11.count_ref, s32[2,16]{1,0:T(2,128)} %bitcast.2, bf16[16,768,384]{2,1,0:T(8,128)(2,1)} %bitcast.5, f32[16,384]{1,0:T(8,128)} %start_ref.1), custom_call_target="tpu_custom_call" | custom-call | flops 9437184 | bytes 9437184 | tf_op jit(solution)/shard_map/first_push/pallas_call | solution.py:180
  12.8 0.0 collective-permute-done.beside_ref
  12.8 0.1 collective-permute-start.1
  12.9 1.3 %collective-permute-done.1 = f32[64,384]{1,0:T(8,128)S(1)} collective-permute-done((f32[64,384]{1,0:T(8,128)S(1)}, f32[64,384]{1,0:T(8,128)S(1)}, u32[]{:S(2)}, u32[]{:S(2)}) %collective-permute-start.1) | collective-permute-done | bytes 98336 | tf_op jit(solution)/shard_map/ppermute | solution.py:54
  14.2 0.3 collective-permute-start.2
  14.5 0.0 collective-permute-start.3
  14.5 4.8 %collective-permute-done.2 = bf16[32,384]{1,0:T(8,128)(2,1)S(1)} collective-permute-done((bf16[32,384]{1,0:T(8,128)(2,1)S(1)}, bf16[32,384]{1,0:T(8,128)(2,1)S(1)}, u32[]{:S(2)}, u32[]{:S(2)}) %collective-permute-start.2) | collective-permute-done | bytes 24608 | tf_op jit(solution)/shard_map/ppermute | solution.py:25
  19.4 0.0 collective-permute-done.3
  19.4 2.5 %collective-permute-start.6 = (bf16[64,384]{1,0:T(8,128)(2,1)S(1)}, bf16[64,384]{1,0:T(8,128)(2,1)S(1)}, u32[]{:S(2)}, u32[]{:S(2)}) collective-permute-start(bf16[64,384]{1,0:T(8,128)(2,1)S(1)} %pad_maximum_fusion.1), channel_id=1, source_target_pairs={{0,28},{4,24},{8,20},{12,16},{16,12},{20,8},{24,4},{28,0},{1,29},{... | collective-permute-start | bytes 147464 | tf_op jit(solution)/shard_map/ppermute | solution.py:68
  21.9 0.3 collective-permute-start.5
  22.1 0.5 collective-permute-start.4
  22.6 1.3 %collective-permute-done.6 = bf16[64,384]{1,0:T(8,128)(2,1)S(1)} collective-permute-done((bf16[64,384]{1,0:T(8,128)(2,1)S(1)}, bf16[64,384]{1,0:T(8,128)(2,1)S(1)}, u32[]{:S(2)}, u32[]{:S(2)}) %collective-permute-start.6) | collective-permute-done | bytes 49184 | tf_op jit(solution)/shard_map/ppermute | solution.py:68
  23.9 1.7 %collective-permute-done.5 = bf16[64,384]{1,0:T(8,128)(2,1)S(1)} collective-permute-done((bf16[64,384]{1,0:T(8,128)(2,1)S(1)}, bf16[64,384]{1,0:T(8,128)(2,1)S(1)}, u32[]{:S(2)}, u32[]{:S(2)}) %collective-permute-start.5) | collective-permute-done | bytes 49184 | tf_op jit(solution)/shard_map/ppermute | solution.py:68
  25.6 0.1 collective-permute-done.4
  25.7 0.0 copy-done.1
  25.7 0.0 copy-done
  25.7 0.0 copy-done.5
  25.7 0.0 copy-done.4
  25.7 0.0 copy-done.3
  25.7 0.0 copy-done.2
  25.7 3.1 %sweep_step.2 = (f32[16,384]{1,0:T(8,128)S(1)}, f32[64,384]{1,0:T(8,128)S(1)}) custom-call(s32[2,16]{1,0:T(2,128)S(1)} %bitcast.3, f32[16,384]{1,0:T(8,128)S(1)} %get-tuple-element.16.live_ref, bf16[16,768,384]{2,1,0:T(8,128)(2,1)S(1)} %get-tuple-element.17.jac_ref, bf16[16,384,768]{2,1,0:T(8,128)(2,1)S(1)} %get-tuple-element.18.turned_ref, ...), custom_call_target="tpu_custom_call" | custom-call | flops 18874368 | bytes 18874368 | tf_op jit(solution)/shard_map/sweep_step/pallas_call | solution.py:206
  28.9 0.4 collective-permute-start.7
  29.3 1.0 %collective-permute-done.7 = f32[64,384]{1,0:T(8,128)S(1)} collective-permute-done((f32[64,384]{1,0:T(8,128)S(1)}, f32[64,384]{1,0:T(8,128)S(1)}, u32[]{:S(2)}, u32[]{:S(2)}) %collective-permute-start.7) | collective-permute-done | bytes 98336 | tf_op jit(solution)/shard_map/ppermute | solution.py:54
  30.3 1.8 %collective-permute-start.8 = (bf16[32,384]{1,0:T(8,128)(2,1)S(1)}, bf16[32,384]{1,0:T(8,128)(2,1)S(1)}, u32[]{:S(2)}, u32[]{:S(2)}) collective-permute-start(bf16[32,384]{1,0:T(8,128)(2,1)S(1)} %get-tuple-element.32), channel_id=1, source_target_pairs={{0,7},{1,6},{2,5},{3,4},{4,3},{5,2},{6,1},{7,0},{8,15},{9,14},{10,... | collective-permute-start | bytes 73736 | tf_op jit(solution)/shard_map/ppermute | solution.py:25
  32.1 0.0 collective-permute-start.9
  32.1 3.4 %collective-permute-done.8 = bf16[32,384]{1,0:T(8,128)(2,1)S(1)} collective-permute-done((bf16[32,384]{1,0:T(8,128)(2,1)S(1)}, bf16[32,384]{1,0:T(8,128)(2,1)S(1)}, u32[]{:S(2)}, u32[]{:S(2)}) %collective-permute-start.8) | collective-permute-done | bytes 24608 | tf_op jit(solution)/shard_map/ppermute | solution.py:25
  35.5 0.5 collective-permute-done.9
  36.0 1.3 %collective-permute-start.12 = (bf16[64,384]{1,0:T(8,128)(2,1)S(1)}, bf16[64,384]{1,0:T(8,128)(2,1)S(1)}, u32[]{:S(2)}, u32[]{:S(2)}) collective-permute-start(bf16[64,384]{1,0:T(8,128)(2,1)S(1)} %pad_maximum_fusion.2), channel_id=1, source_target_pairs={{0,28},{4,24},{8,20},{12,16},{16,12},{20,8},{24,4},{28,0},{1,29},{... | collective-permute-start | bytes 147464 | tf_op jit(solution)/shard_map/ppermute | solution.py:68
  37.3 0.7 %collective-permute-start.11 = (bf16[64,384]{1,0:T(8,128)(2,1)S(1)}, bf16[64,384]{1,0:T(8,128)(2,1)S(1)}, u32[]{:S(2)}, u32[]{:S(2)}) collective-permute-start(bf16[64,384]{1,0:T(8,128)(2,1)S(1)} %pad_maximum_fusion.2), channel_id=1, source_target_pairs={{0,20},{4,16},{8,28},{12,24},{16,4},{20,0},{24,12},{28,8},{1,21},{... | collective-permute-start | bytes 147464 | tf_op jit(solution)/shard_map/ppermute | solution.py:68
  38.0 1.0 %collective-permute-start.10 = (bf16[64,384]{1,0:T(8,128)(2,1)S(1)}, bf16[64,384]{1,0:T(8,128)(2,1)S(1)}, u32[]{:S(2)}, u32[]{:S(2)}) collective-permute-start(bf16[64,384]{1,0:T(8,128)(2,1)S(1)} %pad_maximum_fusion.2), channel_id=1, source_target_pairs={{0,12},{4,8},{8,4},{12,0},{16,28},{20,24},{24,20},{28,16},{1,13},{... | collective-permute-start | bytes 147464 | tf_op jit(solution)/shard_map/ppermute | solution.py:68
  39.0 1.8 %collective-permute-done.12 = bf16[64,384]{1,0:T(8,128)(2,1)S(1)} collective-permute-done((bf16[64,384]{1,0:T(8,128)(2,1)S(1)}, bf16[64,384]{1,0:T(8,128)(2,1)S(1)}, u32[]{:S(2)}, u32[]{:S(2)}) %collective-permute-start.12) | collective-permute-done | bytes 49184 | tf_op jit(solution)/shard_map/ppermute | solution.py:68
  40.8 1.2 %collective-permute-done.11 = bf16[64,384]{1,0:T(8,128)(2,1)S(1)} collective-permute-done((bf16[64,384]{1,0:T(8,128)(2,1)S(1)}, bf16[64,384]{1,0:T(8,128)(2,1)S(1)}, u32[]{:S(2)}, u32[]{:S(2)}) %collective-permute-start.11) | collective-permute-done | bytes 49184 | tf_op jit(solution)/shard_map/ppermute | solution.py:68
  42.0 0.0 collective-permute-done.10
  42.0 3.4 %sweep_step.3 = (f32[16,384]{1,0:T(8,128)}, f32[64,384]{1,0:T(8,128)S(1)}) custom-call(s32[2,16]{1,0:T(2,128)S(1)} %bitcast.4, f32[16,384]{1,0:T(8,128)S(1)} %get-tuple-element.16.live_ref, bf16[16,768,384]{2,1,0:T(8,128)(2,1)S(1)} %get-tuple-element.17.jac_ref, bf16[16,384,768]{2,1,0:T(8,128)(2,1)S(1)} %get-tuple-element.18.turned_ref, ...), custom_call_target="tpu_custom_call" | custom-call | flops 18874368 | bytes 18874368 | tf_op jit(solution)/shard_map/sweep_step/pallas_call | solution.py:206
  45.4 0.1 collective-permute-start.13
  45.5 1.2 %collective-permute-done.13 = f32[64,384]{1,0:T(8,128)S(1)} collective-permute-done((f32[64,384]{1,0:T(8,128)S(1)}, f32[64,384]{1,0:T(8,128)S(1)}, u32[]{:S(2)}, u32[]{:S(2)}) %collective-permute-start.13) | collective-permute-done | bytes 98336 | tf_op jit(solution)/shard_map/ppermute | solution.py:54
  46.8 0.1 collective-permute-start.14
  46.8 5.0 %collective-permute-done.14 = bf16[32,384]{1,0:T(8,128)(2,1)S(1)} collective-permute-done((bf16[32,384]{1,0:T(8,128)(2,1)S(1)}, bf16[32,384]{1,0:T(8,128)(2,1)S(1)}, u32[]{:S(2)}, u32[]{:S(2)}) %collective-permute-start.14) | collective-permute-done | bytes 24608 | tf_op jit(solution)/shard_map/ppermute | solution.py:25
  51.9 1.9 %collective-permute-start.17 = (bf16[32,384]{1,0:T(8,128)(2,1)S(1)}, bf16[32,384]{1,0:T(8,128)(2,1)S(1)}, u32[]{:S(2)}, u32[]{:S(2)}) collective-permute-start(bf16[32,384]{1,0:T(8,128)(2,1)S(1)} %fusion), channel_id=1, source_target_pairs={{0,28},{4,24},{8,20},{12,16},{16,12},{20,8},{24,4},{28,0},{1,29},{... | collective-permute-start | bytes 73736 | tf_op jit(solution)/shard_map/ppermute | solution.py:68
  53.7 0.5 collective-permute-start.16
  54.2 0.7 %collective-permute-start.15 = (bf16[32,384]{1,0:T(8,128)(2,1)S(1)}, bf16[32,384]{1,0:T(8,128)(2,1)S(1)}, u32[]{:S(2)}, u32[]{:S(2)}) collective-permute-start(bf16[32,384]{1,0:T(8,128)(2,1)S(1)} %fusion), channel_id=1, source_target_pairs={{0,12},{4,8},{8,4},{12,0},{16,28},{20,24},{24,20},{28,16},{1,13},{... | collective-permute-start | bytes 73736 | tf_op jit(solution)/shard_map/ppermute | solution.py:68
  54.9 1.2 %collective-permute-done.17 = bf16[32,384]{1,0:T(8,128)(2,1)S(1)} collective-permute-done((bf16[32,384]{1,0:T(8,128)(2,1)S(1)}, bf16[32,384]{1,0:T(8,128)(2,1)S(1)}, u32[]{:S(2)}, u32[]{:S(2)}) %collective-permute-start.17) | collective-permute-done | bytes 24608 | tf_op jit(solution)/shard_map/ppermute | solution.py:68
  56.1 0.9 %collective-permute-done.16 = bf16[32,384]{1,0:T(8,128)(2,1)S(1)} collective-permute-done((bf16[32,384]{1,0:T(8,128)(2,1)S(1)}, bf16[32,384]{1,0:T(8,128)(2,1)S(1)}, u32[]{:S(2)}, u32[]{:S(2)}) %collective-permute-start.16) | collective-permute-done | bytes 24608 | tf_op jit(solution)/shard_map/ppermute | solution.py:68
  57.0 0.5 collective-permute-done.15
  57.5 0.6 %multiply_add_fusion = f32[32,384]{1,0:T(8,128)} fusion(f32[32,384]{1,0:T(8,128)S(1)} %copy-done, f32[32,384]{1,0:T(8,128)S(1)} %copy-done.1, bf16[32,384]{1,0:T(8,128)(2,1)S(1)} %fusion, bf16[32,384]{1,0:T(8,128)(2,1)S(1)} %collective-permute-done.17, bf16[32,384]{1,0:T(8,128)(2,1)S(1)} %collective-permute-done.16, ...), kind=kLoop, calls=%fused_computation.8 | loop fusion | flops 110592 | bytes 245760 | tf_op jit(solution)/shard_map/add | solution.py:246
  (13 shorter events, 0.2 us)
Async XLA Ops:
  0.6 25.0 %copy-start.1 = (f32[32,384]{1,0:T(8,128)S(1)}, f32[32,384]{1,0:T(8,128)}, u32[]{:S(2)}) copy-start(f32[32,384]{1,0:T(8,128)} %mass_ref.3) | copy-start | bytes 147460
  0.6 25.0 %copy-start = (f32[32,384]{1,0:T(8,128)S(1)}, f32[32,384]{1,0:T(8,128)}, u32[]{:S(2)}) copy-start(f32[32,384]{1,0:T(8,128)} %free_ref.3) | copy-start | bytes 147460
  0.7 25.0 %copy-start.5 = (s32[16,2]{0,1:T(2,128)S(1)}, s32[16,2]{0,1:T(2,128)}, u32[]{:S(2)}) copy-start(s32[16,2]{0,1:T(2,128)} %param.10) | copy-start | bytes 388
  0.7 25.0 %copy-start.4 = (f32[16,128]{1,0:T(8,128)S(1)}, f32[16,128]{1,0:T(8,128)}, u32[]{:S(2)}) copy-start(f32[16,128]{1,0:T(8,128)} %friction_ref.3) | copy-start | bytes 24580
  0.7 25.0 %copy-start.3 = (f32[16,384]{1,0:T(8,128)S(1)}, f32[16,384]{1,0:T(8,128)}, u32[]{:S(2)}) copy-start(f32[16,384]{1,0:T(8,128)} %step_ref.3) | copy-start | bytes 73732
  0.7 25.0 %copy-start.2 = (f32[16,384]{1,0:T(8,128)S(1)}, f32[16,384]{1,0:T(8,128)}, u32[]{:S(2)}) copy-start(f32[16,384]{1,0:T(8,128)} %bias_ref.3) | copy-start | bytes 73732
  1.6 11.3 %collective-permute-start = (f32[64,384]{1,0:T(8,128)S(1)}, f32[64,384]{1,0:T(8,128)S(1)}, u32[]{:S(2)}, u32[]{:S(2)}) collective-permute-start(f32[64,384]{1,0:T(8,128)S(1)} %pad_maximum_fusion), channel_id=1, source_target_pairs={{0,3},{1,0},{2,1},{3,2},{4,7},{5,4},{6,5},{7,6},{8,11},{9,8},{10,9... | collective-permute-start | bytes 294920 | tf_op jit(solution)/shard_map/ppermute | solution.py:14
  12.8 1.4 %collective-permute-start.1 = (f32[64,384]{1,0:T(8,128)S(1)}, f32[64,384]{1,0:T(8,128)S(1)}, u32[]{:S(2)}, u32[]{:S(2)}) collective-permute-start(f32[64,384]{1,0:T(8,128)S(1)} %get-tuple-element.22), channel_id=1, source_target_pairs={{0,4},{4,0},{8,12},{12,8},{16,20},{20,16},{24,28},{28,24},{1,5},{5... | collective-permute-start | bytes 294920 | tf_op jit(solution)/shard_map/ppermute | solution.py:54
  14.2 5.1 %collective-permute-start.2 = (bf16[32,384]{1,0:T(8,128)(2,1)S(1)}, bf16[32,384]{1,0:T(8,128)(2,1)S(1)}, u32[]{:S(2)}, u32[]{:S(2)}) collective-permute-start(bf16[32,384]{1,0:T(8,128)(2,1)S(1)} %get-tuple-element.34), channel_id=1, source_target_pairs={{0,7},{1,6},{2,5},{3,4},{4,3},{5,2},{6,1},{7,0},{8,15},{9,14},{10,... | collective-permute-start | bytes 73736 | tf_op jit(solution)/shard_map/ppermute | solution.py:25
  14.5 4.8 %collective-permute-start.3 = (bf16[32,384]{1,0:T(8,128)(2,1)S(1)}, bf16[32,384]{1,0:T(8,128)(2,1)S(1)}, u32[]{:S(2)}, u32[]{:S(2)}) collective-permute-start(bf16[32,384]{1,0:T(8,128)(2,1)S(1)} %get-tuple-element.35), channel_id=1, source_target_pairs={{0,5},{1,4},{2,7},{3,6},{4,1},{5,0},{6,3},{7,2},{8,13},{9,12},{10,... | collective-permute-start | bytes 73736 | tf_op jit(solution)/shard_map/ppermute | solution.py:25
  19.4 4.5 %collective-permute-start.6 = (bf16[64,384]{1,0:T(8,128)(2,1)S(1)}, bf16[64,384]{1,0:T(8,128)(2,1)S(1)}, u32[]{:S(2)}, u32[]{:S(2)}) collective-permute-start(bf16[64,384]{1,0:T(8,128)(2,1)S(1)} %pad_maximum_fusion.1), channel_id=1, source_target_pairs={{0,28},{4,24},{8,20},{12,16},{16,12},{20,8},{24,4},{28,0},{1,29},{... | collective-permute-start | bytes 147464 | tf_op jit(solution)/shard_map/ppermute | solution.py:68
  21.9 3.7 %collective-permute-start.5 = (bf16[64,384]{1,0:T(8,128)(2,1)S(1)}, bf16[64,384]{1,0:T(8,128)(2,1)S(1)}, u32[]{:S(2)}, u32[]{:S(2)}) collective-permute-start(bf16[64,384]{1,0:T(8,128)(2,1)S(1)} %pad_maximum_fusion.1), channel_id=1, source_target_pairs={{0,20},{4,16},{8,28},{12,24},{16,4},{20,0},{24,12},{28,8},{1,21},{... | collective-permute-start | bytes 147464 | tf_op jit(solution)/shard_map/ppermute | solution.py:68
  22.1 3.5 %collective-permute-start.4 = (bf16[64,384]{1,0:T(8,128)(2,1)S(1)}, bf16[64,384]{1,0:T(8,128)(2,1)S(1)}, u32[]{:S(2)}, u32[]{:S(2)}) collective-permute-start(bf16[64,384]{1,0:T(8,128)(2,1)S(1)} %pad_maximum_fusion.1), channel_id=1, source_target_pairs={{0,12},{4,8},{8,4},{12,0},{16,28},{20,24},{24,20},{28,16},{1,13},{... | collective-permute-start | bytes 147464 | tf_op jit(solution)/shard_map/ppermute | solution.py:68
  28.9 1.4 %collective-permute-start.7 = (f32[64,384]{1,0:T(8,128)S(1)}, f32[64,384]{1,0:T(8,128)S(1)}, u32[]{:S(2)}, u32[]{:S(2)}) collective-permute-start(f32[64,384]{1,0:T(8,128)S(1)} %get-tuple-element.25), channel_id=1, source_target_pairs={{0,4},{4,0},{8,12},{12,8},{16,20},{20,16},{24,28},{28,24},{1,5},{5... | collective-permute-start | bytes 294920 | tf_op jit(solution)/shard_map/ppermute | solution.py:54
  30.3 5.2 %collective-permute-start.8 = (bf16[32,384]{1,0:T(8,128)(2,1)S(1)}, bf16[32,384]{1,0:T(8,128)(2,1)S(1)}, u32[]{:S(2)}, u32[]{:S(2)}) collective-permute-start(bf16[32,384]{1,0:T(8,128)(2,1)S(1)} %get-tuple-element.32), channel_id=1, source_target_pairs={{0,7},{1,6},{2,5},{3,4},{4,3},{5,2},{6,1},{7,0},{8,15},{9,14},{10,... | collective-permute-start | bytes 73736 | tf_op jit(solution)/shard_map/ppermute | solution.py:25
  32.1 3.9 %collective-permute-start.9 = (bf16[32,384]{1,0:T(8,128)(2,1)S(1)}, bf16[32,384]{1,0:T(8,128)(2,1)S(1)}, u32[]{:S(2)}, u32[]{:S(2)}) collective-permute-start(bf16[32,384]{1,0:T(8,128)(2,1)S(1)} %get-tuple-element.33), channel_id=1, source_target_pairs={{0,5},{1,4},{2,7},{3,6},{4,1},{5,0},{6,3},{7,2},{8,13},{9,12},{10,... | collective-permute-start | bytes 73736 | tf_op jit(solution)/shard_map/ppermute | solution.py:25
  36.0 4.8 %collective-permute-start.12 = (bf16[64,384]{1,0:T(8,128)(2,1)S(1)}, bf16[64,384]{1,0:T(8,128)(2,1)S(1)}, u32[]{:S(2)}, u32[]{:S(2)}) collective-permute-start(bf16[64,384]{1,0:T(8,128)(2,1)S(1)} %pad_maximum_fusion.2), channel_id=1, source_target_pairs={{0,28},{4,24},{8,20},{12,16},{16,12},{20,8},{24,4},{28,0},{1,29},{... | collective-permute-start | bytes 147464 | tf_op jit(solution)/shard_map/ppermute | solution.py:68
  37.3 4.7 %collective-permute-start.11 = (bf16[64,384]{1,0:T(8,128)(2,1)S(1)}, bf16[64,384]{1,0:T(8,128)(2,1)S(1)}, u32[]{:S(2)}, u32[]{:S(2)}) collective-permute-start(bf16[64,384]{1,0:T(8,128)(2,1)S(1)} %pad_maximum_fusion.2), channel_id=1, source_target_pairs={{0,20},{4,16},{8,28},{12,24},{16,4},{20,0},{24,12},{28,8},{1,21},{... | collective-permute-start | bytes 147464 | tf_op jit(solution)/shard_map/ppermute | solution.py:68
  38.0 4.0 %collective-permute-start.10 = (bf16[64,384]{1,0:T(8,128)(2,1)S(1)}, bf16[64,384]{1,0:T(8,128)(2,1)S(1)}, u32[]{:S(2)}, u32[]{:S(2)}) collective-permute-start(bf16[64,384]{1,0:T(8,128)(2,1)S(1)} %pad_maximum_fusion.2), channel_id=1, source_target_pairs={{0,12},{4,8},{8,4},{12,0},{16,28},{20,24},{24,20},{28,16},{1,13},{... | collective-permute-start | bytes 147464 | tf_op jit(solution)/shard_map/ppermute | solution.py:68
  45.4 1.3 %collective-permute-start.13 = (f32[64,384]{1,0:T(8,128)S(1)}, f32[64,384]{1,0:T(8,128)S(1)}, u32[]{:S(2)}, u32[]{:S(2)}) collective-permute-start(f32[64,384]{1,0:T(8,128)S(1)} %get-tuple-element.27), channel_id=1, source_target_pairs={{0,4},{4,0},{8,12},{12,8},{16,20},{20,16},{24,28},{28,24},{1,5},{5... | collective-permute-start | bytes 294920 | tf_op jit(solution)/shard_map/ppermute | solution.py:54
  46.8 5.1 %collective-permute-start.14 = (bf16[32,384]{1,0:T(8,128)(2,1)S(1)}, bf16[32,384]{1,0:T(8,128)(2,1)S(1)}, u32[]{:S(2)}, u32[]{:S(2)}) collective-permute-start(bf16[32,384]{1,0:T(8,128)(2,1)S(1)} %slice.59), channel_id=1, source_target_pairs={{0,5},{1,6},{2,7},{3,4},{4,1},{5,2},{6,3},{7,0},{8,13},{9,14},{10,... | collective-permute-start | bytes 73736 | tf_op jit(solution)/shard_map/ppermute | solution.py:25
  51.9 4.2 %collective-permute-start.17 = (bf16[32,384]{1,0:T(8,128)(2,1)S(1)}, bf16[32,384]{1,0:T(8,128)(2,1)S(1)}, u32[]{:S(2)}, u32[]{:S(2)}) collective-permute-start(bf16[32,384]{1,0:T(8,128)(2,1)S(1)} %fusion), channel_id=1, source_target_pairs={{0,28},{4,24},{8,20},{12,16},{16,12},{20,8},{24,4},{28,0},{1,29},{... | collective-permute-start | bytes 73736 | tf_op jit(solution)/shard_map/ppermute | solution.py:68
  53.7 3.3 %collective-permute-start.16 = (bf16[32,384]{1,0:T(8,128)(2,1)S(1)}, bf16[32,384]{1,0:T(8,128)(2,1)S(1)}, u32[]{:S(2)}, u32[]{:S(2)}) collective-permute-start(bf16[32,384]{1,0:T(8,128)(2,1)S(1)} %fusion), channel_id=1, source_target_pairs={{0,20},{4,16},{8,28},{12,24},{16,4},{20,0},{24,12},{28,8},{1,21},{... | collective-permute-start | bytes 73736 | tf_op jit(solution)/shard_map/ppermute | solution.py:68
  54.2 3.3 %collective-permute-start.15 = (bf16[32,384]{1,0:T(8,128)(2,1)S(1)}, bf16[32,384]{1,0:T(8,128)(2,1)S(1)}, u32[]{:S(2)}, u32[]{:S(2)}) collective-permute-start(bf16[32,384]{1,0:T(8,128)(2,1)S(1)} %fusion), channel_id=1, source_target_pairs={{0,12},{4,8},{8,4},{12,0},{16,28},{20,24},{24,20},{28,16},{1,13},{... | collective-permute-start | bytes 73736 | tf_op jit(solution)/shard_map/ppermute | solution.py:68
where the time goes:
time: 58.3 us; the launch traced here: 58.1 us
  waiting for transfers between devices  25.8 us (44%)
  starting transfers between devices  17.1 us (29%)
  Pallas kernels  12 us (21%)
  other arithmetic  1.7 us (3%)
  between operations  1.49 us (3%)
    ppermute x5, waiting for transfers between devices, crossed(): return lax.ppermute(value, ('contact', 'body'), pairs)  13.8 us
    ppermute x9, starting transfers between devices, over_pairs(): parts.append(lax.ppermute(rounded(value), 'contact', pairs))  9.26 us
    ppermute x9, waiting for transfers between devices, over_pairs(): parts.append(lax.ppermute(rounded(value), 'contact', pairs))  8.57 us
    pallas_call x2, Pallas kernels, sweep_step(): pl.pallas_call(sweep_kernel, out_shape=result_shapes(lam, blocks, dofs),...  6.53 us
    pallas_call x1, Pallas kernels, first_push(): pl.pallas_call(first_kernel, out_shape=[pltpu.VMEM((tiles, rows, cols), j...  5.5 us
    ppermute x1, starting transfers between devices, shifted(): return lax.ppermute(value, axis, pairs)  5.08 us
    ppermute x3, waiting for transfers between devices, pair_sum(): lax.ppermute(value, 'contact', [(place, place ^ 1) for place in range(cou...  3.43 us
    ppermute x5, starting transfers between devices, crossed(): return lax.ppermute(value, ('contact', 'body'), pairs)  2.15 us
  transfers between devices with their start and end apart: 18, of which 15 were waited for; matrix products, arithmetic and copies ran while one was open for 0% of the time, Pallas kernels for 9%

commit v1 on v0

--- a/solution.py
+++ b/solution.py
@@ -62,12 +62,14 @@
     stride = 2
     while stride < count:
         radix = min(count // stride, 4)
-        parts = []
-        for digit in range(1, radix):
-            pairs = [(place, place ^ (digit * stride) ^ 1) for place in range(count)]
-            parts.append(lax.ppermute(rounded(value), "contact", pairs))
-        parts.append(rounded(value))
-        value = tree([part.astype(jnp.float32) for part in parts])
+        groups = [
+            [base + digit * stride ^ (digit.bit_count() & 1) for digit in range(radix)]
+            for base in range(count)
+            if base // stride % radix == 0
+        ]
+        copies = jnp.broadcast_to(rounded(value), (radix,) + value.shape)
+        parts = lax.all_to_all(copies, "contact", 0, 0, axis_index_groups=groups)
+        value = tree([parts[digit].astype(jnp.float32) for digit in range(radix)])
         stride *= radix
     return value
 

time: 58.3 us -> 65 us (1.11)
  blocking collectives: 0 us -> 24.9 us
  starting transfers between devices: 17.1 us -> 7.16 us
  waiting for transfers between devices: 25.8 us -> 17.3 us
    all_to_all x0 -> x3, blocking collectives: none -> 24.9 us  [over_pairs(): parts = lax.all_to_all(copies, 'contact', 0, 0, axis_index_groups=groups)]
    ppermute x9 -> x0, starting transfers between devices: 9.26 us -> none  [over_pairs(): parts.append(lax.ppermute(rounded(value), 'contact', pairs))]
    ppermute x9 -> x0, waiting for transfers between devices: 8.57 us -> none  [over_pairs(): parts.append(lax.ppermute(rounded(value), 'contact', pairs))]
  transfers between devices with their start and end apart: 18 -> 9, of which waited for: 15 -> 6; matrix products, arithmetic and copies ran while one was open for 0% -> 0% of each run, Pallas kernels for 9% -> 9%
where the time goes in v1:
time: 65 us; the launch traced here: 64.6 us
  blocking collectives  24.9 us (38%)
  waiting for transfers between devices  17.3 us (27%)
  Pallas kernels  12 us (18%)
  starting transfers between devices  7.16 us (11%)
  other arithmetic  1.69 us (3%)
  between operations  1.51 us (2%)
    all_to_all x3, blocking collectives, over_pairs(): parts = lax.all_to_all(copies, 'contact', 0, 0, axis_index_groups=groups)  24.9 us
    ppermute x5, waiting for transfers between devices, crossed(): return lax.ppermute(value, ('contact', 'body'), pairs)  13.4 us
    pallas_call x2, Pallas kernels, sweep_step(): pl.pallas_call(sweep_kernel, out_shape=result_shapes(lam, blocks, dofs),...  6.53 us
    pallas_call x1, Pallas kernels, first_push(): pl.pallas_call(first_kernel, out_shape=[pltpu.VMEM((tiles, rows, cols), j...  5.5 us
    ppermute x1, starting transfers between devices, shifted(): return lax.ppermute(value, axis, pairs)  5.08 us
    ppermute x3, waiting for transfers between devices, pair_sum(): lax.ppermute(value, 'contact', [(place, place ^ 1) for place in range(cou...  3.87 us
    ppermute x5, starting transfers between devices, crossed(): return lax.ppermute(value, ('contact', 'body'), pairs)  1.95 us
  transfers between devices with their start and end apart: 9, of which 6 were waited for; matrix products, arithmetic and copies ran while one was open for 0% of the time, Pallas kernels for 9%

profile of v1, /device:TPU:0, one launch (start us, length us, event | category | flops | bytes accessed | tf_op | source)
XLA Modules:
  0.0 64.6 jit_solution(4265434353426889113)
XLA Ops:
  0.6 0.0 copy-start.1
  0.6 0.0 copy-start
  0.7 0.0 copy-start.5
  0.7 0.0 copy-start.4
  0.7 0.0 copy-start.3
  0.7 0.0 copy-start.2
  0.7 0.9 %pad_maximum_fusion = f32[64,384]{1,0:T(8,128)S(1)} fusion(f32[32,384]{1,0:T(8,128)} %mass_ref.3, f32[32,384]{1,0:T(8,128)} %free_ref.3), kind=kLoop, calls=%fused_computation | loop fusion | flops 24576 | bytes 196608 | tf_op jit(solution)/shard_map/concatenate | solution.py:233
  1.6 5.1 %collective-permute-start = (f32[64,384]{1,0:T(8,128)S(1)}, f32[64,384]{1,0:T(8,128)S(1)}, u32[]{:S(2)}, u32[]{:S(2)}) collective-permute-start(f32[64,384]{1,0:T(8,128)S(1)} %pad_maximum_fusion), channel_id=1, source_target_pairs={{0,3},{1,0},{2,1},{3,2},{4,7},{5,4},{6,5},{7,6},{8,11},{9,8},{10,9... | collective-permute-start | bytes 294920 | tf_op jit(solution)/shard_map/ppermute | solution.py:14
  7.3 5.5 %first_push.1 = (bf16[16,768,384]{2,1,0:T(8,128)(2,1)S(1)}, bf16[16,384,768]{2,1,0:T(8,128)(2,1)S(1)}, f32[16,384]{1,0:T(8,128)S(1)}, f32[16,384]{1,0:T(8,128)S(1)}, f32[64,384]{1,0:T(8,128)S(1)}) custom-call(s32[1]{0:T(128)S(6)} %copy.11.count_ref, s32[2,16]{1,0:T(2,128)} %bitcast.10, bf16[16,768,384]{2,1,0:T(8,128)(2,1)} %bitcast.13, f32[16,384]{1,0:T(8,128)} %start_ref.1), custom_call_target="tpu_custom_call" | custom-call | flops 9437184 | bytes 9437184 | tf_op jit(solution)/shard_map/first_push/pallas_call | solution.py:182
  12.8 0.0 collective-permute-done.beside_ref
  12.8 0.1 collective-permute-start.1
  12.9 1.3 %collective-permute-done.1 = f32[64,384]{1,0:T(8,128)S(1)} collective-permute-done((f32[64,384]{1,0:T(8,128)S(1)}, f32[64,384]{1,0:T(8,128)S(1)}, u32[]{:S(2)}, u32[]{:S(2)}) %collective-permute-start.1) | collective-permute-done | bytes 98336 | tf_op jit(solution)/shard_map/ppermute | solution.py:54
  14.2 0.3 collective-permute-start.2
  14.5 0.0 collective-permute-start.3
  14.5 4.8 %collective-permute-done.2 = bf16[32,384]{1,0:T(8,128)(2,1)S(1)} collective-permute-done((bf16[32,384]{1,0:T(8,128)(2,1)S(1)}, bf16[32,384]{1,0:T(8,128)(2,1)S(1)}, u32[]{:S(2)}, u32[]{:S(2)}) %collective-permute-start.2) | collective-permute-done | bytes 24608 | tf_op jit(solution)/shard_map/ppermute | solution.py:25
  19.4 0.0 collective-permute-done.3
  19.4 9.2 %all_to_all.15 = bf16[4,64,384]{2,1,0:T(8,128)(2,1)S(1)} all-to-all(bf16[4,64,384]{2,1,0:T(8,128)(2,1)S(1)} %broadcast_in_dim.9), channel_id=1, replica_groups={{0,12,20,24},{4,8,16,28},{1,13,21,25},{5,9,17,29},{2,14,22,26},{6,10,18..., dimensions={0} | all-to-all | bytes 393216 | tf_op jit(solution)/shard_map/all_to_all | solution.py:71
  28.7 0.0 copy-done.1
  28.7 0.0 copy-done
  28.7 0.0 copy-done.5
  28.7 0.0 copy-done.4
  28.7 0.0 copy-done.3
  28.7 0.0 copy-done.2
  28.7 3.1 %sweep_step.2 = (f32[16,384]{1,0:T(8,128)S(1)}, f32[64,384]{1,0:T(8,128)S(1)}) custom-call(s32[2,16]{1,0:T(2,128)S(1)} %bitcast.11, f32[16,384]{1,0:T(8,128)S(1)} %get-tuple-element.16.live_ref, bf16[16,768,384]{2,1,0:T(8,128)(2,1)S(1)} %get-tuple-element.17.jac_ref, bf16[16,384,768]{2,1,0:T(8,128)(2,1)S(1)} %get-tuple-element.18.turned_ref, ...), custom_call_target="tpu_custom_call" | custom-call | flops 18874368 | bytes 18874368 | tf_op jit(solution)/shard_map/sweep_step/pallas_call | solution.py:208
  31.9 0.1 collective-permute-start.4
  31.9 1.3 %collective-permute-done.4 = f32[64,384]{1,0:T(8,128)S(1)} collective-permute-done((f32[64,384]{1,0:T(8,128)S(1)}, f32[64,384]{1,0:T(8,128)S(1)}, u32[]{:S(2)}, u32[]{:S(2)}) %collective-permute-start.4) | collective-permute-done | bytes 98336 | tf_op jit(solution)/shard_map/ppermute | solution.py:54
  33.2 1.6 %collective-permute-start.5 = (bf16[32,384]{1,0:T(8,128)(2,1)S(1)}, bf16[32,384]{1,0:T(8,128)(2,1)S(1)}, u32[]{:S(2)}, u32[]{:S(2)}) collective-permute-start(bf16[32,384]{1,0:T(8,128)(2,1)S(1)} %get-tuple-element.32), channel_id=1, source_target_pairs={{0,7},{1,6},{2,5},{3,4},{4,3},{5,2},{6,1},{7,0},{8,15},{9,14},{10,... | collective-permute-start | bytes 73736 | tf_op jit(solution)/shard_map/ppermute | solution.py:25
  34.9 0.0 collective-permute-start.6
  34.9 3.5 %collective-permute-done.5 = bf16[32,384]{1,0:T(8,128)(2,1)S(1)} collective-permute-done((bf16[32,384]{1,0:T(8,128)(2,1)S(1)}, bf16[32,384]{1,0:T(8,128)(2,1)S(1)}, u32[]{:S(2)}, u32[]{:S(2)}) %collective-permute-start.5) | collective-permute-done | bytes 24608 | tf_op jit(solution)/shard_map/ppermute | solution.py:25
  38.4 0.0 collective-permute-done.6
  38.5 8.3 %all_to_all.16 = bf16[4,64,384]{2,1,0:T(8,128)(2,1)S(1)} all-to-all(bf16[4,64,384]{2,1,0:T(8,128)(2,1)S(1)} %broadcast_in_dim.10), channel_id=1, replica_groups={{0,12,20,24},{4,8,16,28},{1,13,21,25},{5,9,17,29},{2,14,22,26},{6,10,18..., dimensions={0} | all-to-all | bytes 393216 | tf_op jit(solution)/shard_map/all_to_all | solution.py:71
  46.8 3.4 %sweep_step.3 = (f32[16,384]{1,0:T(8,128)}, f32[64,384]{1,0:T(8,128)S(1)}) custom-call(s32[2,16]{1,0:T(2,128)S(1)} %bitcast.12, f32[16,384]{1,0:T(8,128)S(1)} %get-tuple-element.16.live_ref, bf16[16,768,384]{2,1,0:T(8,128)(2,1)S(1)} %get-tuple-element.17.jac_ref, bf16[16,384,768]{2,1,0:T(8,128)(2,1)S(1)} %get-tuple-element.18.turned_ref, ...), custom_call_target="tpu_custom_call" | custom-call | flops 18874368 | bytes 18874368 | tf_op jit(solution)/shard_map/sweep_step/pallas_call | solution.py:208
  50.2 0.0 collective-permute-start.7
  50.2 1.3 %collective-permute-done.7 = f32[64,384]{1,0:T(8,128)S(1)} collective-permute-done((f32[64,384]{1,0:T(8,128)S(1)}, f32[64,384]{1,0:T(8,128)S(1)}, u32[]{:S(2)}, u32[]{:S(2)}) %collective-permute-start.7) | collective-permute-done | bytes 98336 | tf_op jit(solution)/shard_map/ppermute | solution.py:54
  51.6 0.1 collective-permute-start.8
  51.6 5.0 %collective-permute-done.8 = bf16[32,384]{1,0:T(8,128)(2,1)S(1)} collective-permute-done((bf16[32,384]{1,0:T(8,128)(2,1)S(1)}, bf16[32,384]{1,0:T(8,128)(2,1)S(1)}, u32[]{:S(2)}, u32[]{:S(2)}) %collective-permute-start.8) | collective-permute-done | bytes 24608 | tf_op jit(solution)/shard_map/ppermute | solution.py:25
  56.7 7.3 %all_to_all.17 = bf16[4,32,384]{2,1,0:T(8,128)(2,1)S(1)} all-to-all(bf16[4,32,384]{2,1,0:T(8,128)(2,1)S(1)} %broadcast_in_dim.11), channel_id=1, replica_groups={{0,12,20,24},{4,8,16,28},{1,13,21,25},{5,9,17,29},{2,14,22,26},{6,10,18..., dimensions={0} | all-to-all | bytes 196608 | tf_op jit(solution)/shard_map/all_to_all | solution.py:71
  64.0 0.6 fusion.1
  (16 shorter events, 0.2 us)
Async XLA Ops:
  0.6 28.0 %copy-start.1 = (f32[32,384]{1,0:T(8,128)S(1)}, f32[32,384]{1,0:T(8,128)}, u32[]{:S(2)}) copy-start(f32[32,384]{1,0:T(8,128)} %mass_ref.3) | copy-start | bytes 147460
  0.6 28.0 %copy-start = (f32[32,384]{1,0:T(8,128)S(1)}, f32[32,384]{1,0:T(8,128)}, u32[]{:S(2)}) copy-start(f32[32,384]{1,0:T(8,128)} %free_ref.3) | copy-start | bytes 147460
  0.7 28.0 %copy-start.5 = (s32[16,2]{0,1:T(2,128)S(1)}, s32[16,2]{0,1:T(2,128)}, u32[]{:S(2)}) copy-start(s32[16,2]{0,1:T(2,128)} %param.10) | copy-start | bytes 388
  0.7 28.0 %copy-start.4 = (f32[16,128]{1,0:T(8,128)S(1)}, f32[16,128]{1,0:T(8,128)}, u32[]{:S(2)}) copy-start(f32[16,128]{1,0:T(8,128)} %friction_ref.3) | copy-start | bytes 24580
  0.7 28.0 %copy-start.3 = (f32[16,384]{1,0:T(8,128)S(1)}, f32[16,384]{1,0:T(8,128)}, u32[]{:S(2)}) copy-start(f32[16,384]{1,0:T(8,128)} %step_ref.3) | copy-start | bytes 73732
  0.7 28.0 %copy-start.2 = (f32[16,384]{1,0:T(8,128)S(1)}, f32[16,384]{1,0:T(8,128)}, u32[]{:S(2)}) copy-start(f32[16,384]{1,0:T(8,128)} %bias_ref.3) | copy-start | bytes 73732
  1.6 11.3 %collective-permute-start = (f32[64,384]{1,0:T(8,128)S(1)}, f32[64,384]{1,0:T(8,128)S(1)}, u32[]{:S(2)}, u32[]{:S(2)}) collective-permute-start(f32[64,384]{1,0:T(8,128)S(1)} %pad_maximum_fusion), channel_id=1, source_target_pairs={{0,3},{1,0},{2,1},{3,2},{4,7},{5,4},{6,5},{7,6},{8,11},{9,8},{10,9... | collective-permute-start | bytes 294920 | tf_op jit(solution)/shard_map/ppermute | solution.py:14
  12.8 1.4 %collective-permute-start.1 = (f32[64,384]{1,0:T(8,128)S(1)}, f32[64,384]{1,0:T(8,128)S(1)}, u32[]{:S(2)}, u32[]{:S(2)}) collective-permute-start(f32[64,384]{1,0:T(8,128)S(1)} %get-tuple-element.22), channel_id=1, source_target_pairs={{0,4},{4,0},{8,12},{12,8},{16,20},{20,16},{24,28},{28,24},{1,5},{5... | collective-permute-start | bytes 294920 | tf_op jit(solution)/shard_map/ppermute | solution.py:54
  14.2 5.1 %collective-permute-start.2 = (bf16[32,384]{1,0:T(8,128)(2,1)S(1)}, bf16[32,384]{1,0:T(8,128)(2,1)S(1)}, u32[]{:S(2)}, u32[]{:S(2)}) collective-permute-start(bf16[32,384]{1,0:T(8,128)(2,1)S(1)} %get-tuple-element.34), channel_id=1, source_target_pairs={{0,7},{1,6},{2,5},{3,4},{4,3},{5,2},{6,1},{7,0},{8,15},{9,14},{10,... | collective-permute-start | bytes 73736 | tf_op jit(solution)/shard_map/ppermute | solution.py:25
  14.5 4.8 %collective-permute-start.3 = (bf16[32,384]{1,0:T(8,128)(2,1)S(1)}, bf16[32,384]{1,0:T(8,128)(2,1)S(1)}, u32[]{:S(2)}, u32[]{:S(2)}) collective-permute-start(bf16[32,384]{1,0:T(8,128)(2,1)S(1)} %get-tuple-element.35), channel_id=1, source_target_pairs={{0,5},{1,4},{2,7},{3,6},{4,1},{5,0},{6,3},{7,2},{8,13},{9,12},{10,... | collective-permute-start | bytes 73736 | tf_op jit(solution)/shard_map/ppermute | solution.py:25
  31.9 1.4 %collective-permute-start.4 = (f32[64,384]{1,0:T(8,128)S(1)}, f32[64,384]{1,0:T(8,128)S(1)}, u32[]{:S(2)}, u32[]{:S(2)}) collective-permute-start(f32[64,384]{1,0:T(8,128)S(1)} %get-tuple-element.25), channel_id=1, source_target_pairs={{0,4},{4,0},{8,12},{12,8},{16,20},{20,16},{24,28},{28,24},{1,5},{5... | collective-permute-start | bytes 294920 | tf_op jit(solution)/shard_map/ppermute | solution.py:54
  33.2 5.1 %collective-permute-start.5 = (bf16[32,384]{1,0:T(8,128)(2,1)S(1)}, bf16[32,384]{1,0:T(8,128)(2,1)S(1)}, u32[]{:S(2)}, u32[]{:S(2)}) collective-permute-start(bf16[32,384]{1,0:T(8,128)(2,1)S(1)} %get-tuple-element.32), channel_id=1, source_target_pairs={{0,7},{1,6},{2,5},{3,4},{4,3},{5,2},{6,1},{7,0},{8,15},{9,14},{10,... | collective-permute-start | bytes 73736 | tf_op jit(solution)/shard_map/ppermute | solution.py:25
  34.9 3.5 %collective-permute-start.6 = (bf16[32,384]{1,0:T(8,128)(2,1)S(1)}, bf16[32,384]{1,0:T(8,128)(2,1)S(1)}, u32[]{:S(2)}, u32[]{:S(2)}) collective-permute-start(bf16[32,384]{1,0:T(8,128)(2,1)S(1)} %get-tuple-element.33), channel_id=1, source_target_pairs={{0,5},{1,4},{2,7},{3,6},{4,1},{5,0},{6,3},{7,2},{8,13},{9,12},{10,... | collective-permute-start | bytes 73736 | tf_op jit(solution)/shard_map/ppermute | solution.py:25
  50.2 1.3 %collective-permute-start.7 = (f32[64,384]{1,0:T(8,128)S(1)}, f32[64,384]{1,0:T(8,128)S(1)}, u32[]{:S(2)}, u32[]{:S(2)}) collective-permute-start(f32[64,384]{1,0:T(8,128)S(1)} %get-tuple-element.27), channel_id=1, source_target_pairs={{0,4},{4,0},{8,12},{12,8},{16,20},{20,16},{24,28},{28,24},{1,5},{5... | collective-permute-start | bytes 294920 | tf_op jit(solution)/shard_map/ppermute | solution.py:54
  51.6 5.1 %collective-permute-start.8 = (bf16[32,384]{1,0:T(8,128)(2,1)S(1)}, bf16[32,384]{1,0:T(8,128)(2,1)S(1)}, u32[]{:S(2)}, u32[]{:S(2)}) collective-permute-start(bf16[32,384]{1,0:T(8,128)(2,1)S(1)} %slice.131), channel_id=1, source_target_pairs={{0,5},{1,6},{2,7},{3,4},{4,1},{5,2},{6,3},{7,0},{8,13},{9,14},{10,... | collective-permute-start | bytes 73736 | tf_op jit(solution)/shard_map/ppermute | solution.py:25
